TPU v7x, 32 devices: a whole 2x2x4 slice. The times are simulated.
32 devices in a mesh: band: 4 (over y, x), dom: 8 (over z, core).
Axes of the slice: x: 2, y: 2, z: 4, core: 2. Of those that a mesh axis runs over, the one named last changes fastest.
Arguments:
- orbitals: bfloat16 [256, 64, 2048], P('dom', None, 'band'), may hold values from -6 to 6
- projector_blocks: bfloat16 [4, 8, 96, 256, 128], P('band', 'dom'), may hold values from -0.1875 to 0.1875
- block_rows: int32 [4, 8, 96], P('band', 'dom'), may hold values from 0 to 15, as said below
- block_cols: int32 [4, 8, 96], P('band', 'dom'), may hold values from 0 to 26
- block_counts: int32 [4, 8], P('band', 'dom'), may hold values from 16 to 96, as said below
- strengths: float32 [9216], P('dom'), may hold values from -1.5 to 1.5
Outputs:
- applied: bfloat16 [256, 64, 2048], P('dom', None, 'band')
Inputs may be any that keep to these rules, and one draw needn't show every extreme that they name: `block_rows`: the slots of one device name distinct pairs of row block and column block. `block_counts`: some device has all 96 slots live.
All inputs are finite; a program needn't handle non-finite values.
Results may differ from a plain program's by a relative error of at most 0.0049.
Values may be sent and summed in bfloat16 or wider, within the bound.
No kernel may reach another device: no remote copies, remote signals or barrier semaphores. Data moves between devices by JAX's collectives and lax.ppermute only.
A program may use at most 128 MiB of HBM per device.

v0:
```python
import jax
import jax.numpy as jnp
from jax import lax
from jax.sharding import PartitionSpec as P


def passed_along(value, axis, steps):
    count = lax.axis_size(axis)
    pairs = [(source, (source + steps) % count) for source in range(count)]
    return lax.ppermute(value, axis, pairs)


def padded(shard, sides, width):
    for axis, dim in sides:
        size, length = (lax.axis_size(axis), shard.shape[dim])
        up = [(i, (i + 1) % size) for i in range(size)]
        down = [(j, i) for i, j in up]
        last = lax.slice_in_dim(shard, length - width, length, axis=dim)
        leading = lax.slice_in_dim(shard, 0, width, axis=dim)
        before = lax.ppermute(last, axis, up)
        after = lax.ppermute(leading, axis, down)
        shard = jnp.concatenate([before, shard, after], axis=dim)
    return shard


def per_device(orbitals, projector_blocks, block_rows, block_cols, block_counts, strengths):
    slab_states = lax.all_to_all(orbitals, "dom", split_axis=1, concat_axis=0, tiled=True)
    state_total = slab_states.shape[0]
    planes = slab_states.shape[1]
    points = slab_states.shape[2]
    weights = projector_blocks[0, 0]
    slot_total = weights.shape[0]
    row_width = weights.shape[1]
    col_width = weights.shape[2]
    row_blocks = planes * points // row_width
    col_blocks = strengths.shape[0] // col_width
    slot_rows = block_rows[0, 0]
    slot_cols = block_cols[0, 0]
    live_total = block_counts[0, 0]
    live_weight = (jnp.arange(slot_total, dtype=jnp.int32) < live_total).astype(jnp.float32)
    picked = jnp.take(slab_states.reshape(state_total, row_blocks, row_width), slot_rows, axis=1)
    projected = jnp.einsum("skr,krc->kcs", picked, weights, preferred_element_type=jnp.float32)
    projected = projected * live_weight[:, None, None]
    partial_value = (
        jnp.zeros((3 * col_blocks, col_width, state_total), jnp.float32)
        .at[slot_cols]
        .add(projected)
    )
    partial_value = partial_value.reshape(3, col_blocks, col_width, state_total)
    scaling = strengths.reshape(col_blocks, col_width, 1)
    summed = lax.psum(partial_value, "band")
    below_part = passed_along(summed[2], "dom", 1)
    above_part = passed_along(summed[0], "dom", -1)
    scaled = (scaling * (summed[1] + below_part + above_part)).astype(jnp.bfloat16)
    neighbours = padded(scaled[None], (("dom", 0),), 1)
    neighbours = neighbours.reshape(3 * col_blocks, col_width, state_total)
    selected = jnp.take(neighbours, slot_cols, axis=0)
    returned = jnp.einsum("krc,kcs->skr", weights, selected, preferred_element_type=jnp.float32)
    returned = returned * live_weight[None, :, None]
    placed = (
        jnp.zeros((state_total, row_blocks, row_width), jnp.float32)
        .at[:, slot_rows, :]
        .add(returned)
    )
    result = placed.astype(jnp.bfloat16).reshape(state_total, planes, points)
    return lax.all_to_all(result, "dom", split_axis=0, concat_axis=1, tiled=True)


def solution(mesh):
    return jax.shard_map(
        per_device,
        mesh=mesh,
        in_specs=(
            P("dom", None, "band"),
            P("band", "dom", None, None, None),
            P("band", "dom", None),
            P("band", "dom", None),
            P("band", "dom"),
            P("dom"),
        ),
        out_specs=P("dom", None, "band"),
        check_vma=False,
    )
```

profile of v0, /device:TPU:0, one launch (start us, length us, event | category | flops | bytes accessed | tf_op | source)
XLA Modules:
  0.0 416.2 jit_solution(10674326411382505007)
XLA Ops:
  6.5 4.1 copy.21
  10.6 6.3 %all-to-all-start = ((bf16[32,64,512]{2,0,1:T(8,128)(2,1)}), bf16[32,64,512]{2,0,1:T(8,128)(2,1)S(1)}, u32[]{:S(2)}, u32[]{:S(2)}) async-start(bf16[32,64,512]{2,0,1:T(8,128)(2,1)} %copy.21), calls=%async_computation | async-start | bytes 4194304 | tf_op jit(solution)/shard_map/all_to_all | solution.py:27
  17.7 0.5 copy-done.2
  18.3 47.8 %all-to-all-done = bf16[32,64,512]{2,0,1:T(8,128)(2,1)S(1)} async-done(((bf16[32,64,512]{2,0,1:T(8,128)(2,1)}), bf16[32,64,512]{2,0,1:T(8,128)(2,1)S(1)}, u32[]{:S(2)}, u32[]{:S(2)}) %all-to-all-start) | async-done | bytes 2097184 | tf_op jit(solution)/shard_map/all_to_all | solution.py:27
  66.0 2.6 copy.33
  68.6 4.1 reshape.93
  72.6 2.3 copy.23
  74.9 6.8 %gather_fusion = bf16[96,256,256]{2,1,0:T(8,128)(2,1)} fusion(bf16[256,16,256]{2,0,1:T(8,128)(2,1)S(1)} %copy.23, s32[1024]{0:T(1024)S(1)} %pad_clamp_fusion.1), kind=kCustom, calls=%fused_computation | custom fusion | bytes 25166208 | tf_op jit(solution)/shard_map/jit(_take)/gather | solution.py:41
  81.7 14.4 %multiply_bitcast_fusion = f32[96,128,256]{1,2,0:T(8,128)} fusion(f32[96]{0:T(128)S(1)} %get-tuple-element.7, bf16[1,1,96,256,128]{4,3,2,1,0:T(8,128)(2,1)} %param.7, bf16[96,256,256]{2,1,0:T(8,128)(2,1)} %gather_fusion, pred[96]{0:T(512)(128)(4,1)S(1)} %get-tuple-element.8), kind=kOutput, calls=%fused_computation.8 | convolution fusion | flops 1620049920 | bytes 31457760 | tf_op jit(solution)/shard_map/skr,krc->kcs/dot_general | solution.py:42
  96.1 12.6 %copy.24 = f32[96,128,256]{2,1,0:T(8,128)} copy(f32[96,128,256]{1,2,0:T(8,128)} %multiply_bitcast_fusion) | data formatting | bytes 25165824 | tf_op jit(solution)/shard_map/mul | solution.py:43
  108.7 0.4 broadcast_in_dim.35
  109.1 18.4 %scatter_fusion = f32[27,128,256]{2,1,0:T(8,128)S(1)} fusion(f32[27,128,256]{2,1,0:T(8,128)S(1)} %broadcast_in_dim.35, s32[96]{0:T(128)S(1)} %fusion.23, f32[96,128,256]{2,1,0:T(8,128)} %copy.24), kind=kCustom, calls=%fused_computation.2 | custom fusion | flops 3145728 | bytes 37749120 | tf_op jit(solution)/shard_map/scatter-add | solution.py:47
  127.6 1.8 copy-done
  129.4 92.8 %all-reduce.2.cloned.1.call-done = f32[3,9,128,256]{3,2,1,0:T(8,128)} async-done(((f32[3,9,128,256]{3,2,1,0:T(8,128)}), f32[3,9,128,256]{3,2,1,0:T(8,128)}) %all-reduce.2.cloned.1.call-update) | async-done | bytes 3538960 | tf_op jit(solution)/shard_map/psum | solution.py:51
  222.2 1.8 slice_bitcast_fusion.1
  224.0 0.1 collective-permute-start
  224.1 3.5 collective-permute-start.1
  227.6 24.6 %collective-permute-done = f32[9,128,256]{2,1,0:T(8,128)S(1)} collective-permute-done((f32[9,128,256]{2,1,0:T(8,128)S(1)}, f32[9,128,256]{2,1,0:T(8,128)S(1)}, u32[]{:S(2)}, u32[]{:S(2)}) %collective-permute-start) | collective-permute-done | bytes 1179680 | tf_op jit(solution)/shard_map/ppermute | solution.py:10
  252.3 1.6 fusion.21
  253.8 1.7 collective-permute-start.2
  255.6 1.9 collective-permute-start.3
  257.5 13.5 %collective-permute-done.2 = bf16[1,9,128,256]{3,2,1,0:T(8,128)(2,1)S(1)} collective-permute-done((bf16[1,9,128,256]{3,2,1,0:T(8,128)(2,1)S(1)}, bf16[1,9,128,256]{3,2,1,0:T(8,128)(2,1)S(1)}, u32[]{:S(2)}, u32[]{:S(2)}) %collective-permute-start.2) | collective-permute-done | bytes 589856 | tf_op jit(solution)/shard_map/ppermute | solution.py:20
  271.0 0.2 pad_maximum_fusion
  271.2 6.0 %gather_fusion.1 = bf16[96,128,256]{2,1,0:T(8,128)(2,1)} fusion(bf16[27,128,256]{2,1,0:T(8,128)(2,1)S(1)} %bitcast.65, s32[1024]{0:T(1024)S(1)} %pad_clamp_fusion), kind=kCustom, calls=%fused_computation.1 | custom fusion | bytes 12583296 | tf_op jit(solution)/shard_map/jit(_take)/gather | solution.py:57
  277.2 14.3 %broadcast_multiply_fusion = f32[96,256,256]{2,1,0:T(8,128)} fusion(f32[96]{0:T(128)S(1)} %get-tuple-element.7, bf16[1,1,96,256,128]{4,3,2,1,0:T(8,128)(2,1)} %param.7, bf16[96,128,256]{2,1,0:T(8,128)(2,1)} %gather_fusion.1, pred[96]{0:T(512)(128)(4,1)S(1)} %compare_and_fusion.1), kind=kOutput, calls=%fused_computation.7 | convolution fusion | flops 1620049920 | bytes 37749216 | tf_op jit(solution)/shard_map/krc,kcs->skr/dot_general | solution.py:58
  291.5 2.4 broadcast_in_dim.33
  293.9 54.2 %scatter_fusion.1 = f32[256,16,256]{2,0,1:T(8,128)} fusion(f32[256,16,256]{2,0,1:T(8,128)} %broadcast_in_dim.33, s32[96]{0:T(128)S(1)} %copy-done.3, f32[96,256,256]{2,1,0:T(8,128)} %broadcast_multiply_fusion), kind=kCustom, calls=%fused_computation.3 | custom fusion | flops 6291456 | bytes 75497856 | tf_op jit(solution)/shard_map/scatter-add | solution.py:63
  348.1 2.4 convert_element_type.19
  350.5 2.4 copy.26
  352.9 3.4 copy.27
  356.3 51.5 %all_to_all.33 = bf16[256,8,512]{2,1,0:T(8,128)(2,1)S(1)} all-to-all(bf16[256,8,512]{2,1,0:T(8,128)(2,1)S(1)} %copy.27), channel_id=1, replica_groups=mesh['band'=4,'dom'=8] {'dom'}, dimensions={0} | all-to-all | bytes 4194304 | tf_op jit(solution)/shard_map/all_to_all | solution.py:66
  407.8 1.6 copy.32
  (22 shorter events, 0.1 us)
Async XLA Ops:
  6.5 11.1 %copy-start.4 = (s32[1,1,96]{2,1,0:T(1,128)S(1)}, s32[1,1,96]{2,1,0:T(1,128)}, u32[]{:S(2)}) copy-start(s32[1,1,96]{2,1,0:T(1,128)} %param.8) | copy-start | bytes 1156
  6.5 11.2 %copy-start.5 = (s32[1,1,96]{2,1,0:T(1,128)S(1)}, s32[1,1,96]{2,1,0:T(1,128)}, u32[]{:S(2)}) copy-start(s32[1,1,96]{2,1,0:T(1,128)} %param.9) | copy-start | bytes 1156
  10.6 55.4 %all-to-all-start = ((bf16[32,64,512]{2,0,1:T(8,128)(2,1)}), bf16[32,64,512]{2,0,1:T(8,128)(2,1)S(1)}, u32[]{:S(2)}, u32[]{:S(2)}) async-start(bf16[32,64,512]{2,0,1:T(8,128)(2,1)} %copy.21), calls=%async_computation | async-start | bytes 4194304 | tf_op jit(solution)/shard_map/all_to_all | solution.py:27
  17.0 205.2 %all-reduce.2.cloned.1.call-start = ((), (), s32[]{:S(2)}) async-start(), calls=%async_computation.2 | async-start | bytes 7077888 | tf_op jit(solution)/shard_map/psum | solution.py:51
  17.7 0.6 copy-start.2
  127.5 1.8 copy-start
  127.5 124.7 %copy-start.1 = (f32[1152]{0:T(1024)S(1)}, f32[1152]{0:T(1024)}, u32[]{:S(2)}) copy-start(f32[1152]{0:T(1024)} %param.11) | copy-start | bytes 13828
  129.4 128.1 %copy-start.6 = (s32[1,1,96]{2,1,0:T(1,128)S(1)}, s32[1,1,96]{2,1,0:T(1,128)}, u32[]{:S(2)}) copy-start(s32[1,1,96]{2,1,0:T(1,128)} %param.9) | copy-start | bytes 1156
  224.0 28.2 %collective-permute-start = (f32[9,128,256]{2,1,0:T(8,128)S(1)}, f32[9,128,256]{2,1,0:T(8,128)S(1)}, u32[]{:S(2)}, u32[]{:S(2)}) collective-permute-start(f32[9,128,256]{2,1,0:T(8,128)S(1)} %get-tuple-element.5), channel_id=1, source_target_pairs={{0,1},{1,2},{2,3},{3,4},{4,5},{5,6},{6,7},{7,0},{8,9},{9,10},{10,1... | collective-permute-start | bytes 3538952 | tf_op jit(solution)/shard_map/ppermute | solution.py:10
  224.1 28.2 %collective-permute-start.1 = (f32[9,128,256]{2,1,0:T(8,128)S(1)}, f32[9,128,256]{2,1,0:T(8,128)S(1)}, u32[]{:S(2)}, u32[]{:S(2)}) collective-permute-start(f32[9,128,256]{2,1,0:T(8,128)S(1)} %get-tuple-element.6), channel_id=1, source_target_pairs={{0,7},{1,0},{2,1},{3,2},{4,3},{5,4},{6,5},{7,6},{8,15},{9,8},{10,9... | collective-permute-start | bytes 3538952 | tf_op jit(solution)/shard_map/ppermute | solution.py:10
  253.8 17.1 %collective-permute-start.2 = (bf16[1,9,128,256]{3,2,1,0:T(8,128)(2,1)S(1)}, bf16[1,9,128,256]{3,2,1,0:T(8,128)(2,1)S(1)}, u32[]{:S(2)}, u32[]{:S(2)}) collective-permute-start(bf16[1,9,128,256]{3,2,1,0:T(8,128)(2,1)S(1)} %fusion.21), channel_id=1, source_target_pairs={{0,1},{1,2},{2,3},{3,4},{4,5},{5,6},{6,7},{7,0},{8,9},{9,10},{10,1... | collective-permute-start | bytes 1769480 | tf_op jit(solution)/shard_map/ppermute | solution.py:20
  255.6 15.4 %collective-permute-start.3 = (bf16[1,9,128,256]{3,2,1,0:T(8,128)(2,1)S(1)}, bf16[1,9,128,256]{3,2,1,0:T(8,128)(2,1)S(1)}, u32[]{:S(2)}, u32[]{:S(2)}) collective-permute-start(bf16[1,9,128,256]{3,2,1,0:T(8,128)(2,1)S(1)} %fusion.21), channel_id=1, source_target_pairs={{1,0},{2,1},{3,2},{4,3},{5,4},{6,5},{7,6},{0,7},{9,8},{10,9},{11,1... | collective-permute-start | bytes 1769480 | tf_op jit(solution)/shard_map/ppermute | solution.py:21
  291.5 2.4 copy-start.3
Sparse Core Ops, SparseCore 0:
  129.5 92.6 all-reduce.1
where the time goes:
time: 417 us; the launch traced here: 416 us
  waiting for transfers between devices  179 us (43%)
  other arithmetic  76.8 us (18%)
  local copies, waits for them, and re-layouts  52.7 us (13%)
  blocking collectives  51.5 us (12%)
  matrix products  28.7 us (7%)
  between operations  14.2 us (3%)
  starting transfers between devices  13.5 us (3%)
    psum x1, waiting for transfers between devices, per_device(): summed = lax.psum(partial_value, 'band')  92.8 us
    scatter-add x1, other arithmetic, per_device(): placed = jnp.zeros((state_total, row_blocks, row_width), jnp.float32).at[...  54.2 us
    all_to_all x1, blocking collectives, per_device(): lax.all_to_all(result, 'dom', split_axis=0, concat_axis=1, tiled=True)  51.5 us
    all_to_all x1, waiting for transfers between devices, per_device(): lax.all_to_all(orbitals, 'dom', split_axis=1, concat_axis=0, tiled=True)  47.8 us
    ppermute x2, waiting for transfers between devices, passed_along(): return lax.ppermute(value, axis, pairs)  24.6 us
    scatter-add x1, other arithmetic, per_device(): partial_value = jnp.zeros((3 * col_blocks, col_width, state_total), jnp.f...  18.4 us
    dot_general x1, matrix products, per_device(): jnp.einsum('skr,krc->kcs', picked, weights, preferred_element_type=jnp.fl...  14.4 us
    dot_general x1, matrix products, per_device(): jnp.einsum('krc,kcs->skr', weights, selected, preferred_element_type=jnp....  14.3 us
  transfers between devices with their start and end apart: 6, of which 4 were waited for; matrix products, arithmetic and copies ran while one was open for 0% of the time, Pallas kernels for 0%

commit v1 on v0

v1 whole, which is shorter than its diff:
```python
import jax
import jax.numpy as jnp
from jax import lax
from jax.experimental import pallas as pl
from jax.experimental.pallas import tpu as pltpu
from jax.sharding import PartitionSpec as P

CHUNKS = (16, 16)
DIRECT = True
VMEM_BYTES = 48 * 1024 * 1024
WHOLE = pl.BlockSpec(memory_space=pltpu.VMEM)
SCALARS = pl.BlockSpec(memory_space=pltpu.SMEM)
ANYWHERE = pl.BlockSpec(memory_space=pl.ANY)
CORES = 2


def shifted(value, axis, steps):
    count = lax.axis_size(axis)
    return lax.ppermute(value, axis, [(i, (i + steps) % count) for i in range(count)])


def swapped(value, axis, mask):
    count = lax.axis_size(axis)
    return lax.ppermute(value, axis, [(i, i ^ mask) for i in range(count)])


def each_live(sources, blocks, sems, live, body, width):
    per = sems.shape[1]
    slots = blocks.shape[1]
    step = slots // per

    def copy(side, i):
        span = pl.ds(i * step, step)
        return pltpu.make_async_copy(sources[side].at[span], blocks.at[side, span], sems.at[side, i])

    order = [(side, i) for side in range(len(sources)) for i in range(per)]
    for side, i in order:

        @pl.when(live[side] > i * step)
        def _():
            copy(side, i).start()

    yield
    for side, i in order:
        first = i * step
        here = jnp.clip(live[side] - first, 0, step)
        groups = here // width

        @pl.when(here > 0)
        def _():
            copy(side, i).wait()

        @pl.loop(0, groups)
        def _(g):
            body(side, [first + g * width + t for t in range(width)])

        @pl.loop(groups * width, here)
        def _(k):
            body(side, [first + k])

    yield


def make_project(part_total):
    def kernel(rows, cols, live, origin, *rest):
        parts, rest = rest[:part_total], rest[part_total:]
        sources, after, outs = rest[:CORES], rest[CORES], rest[CORES + 1 : -3]
        blocks, total, sems = rest[-3:]
        width = blocks.shape[2]
        halves = parts[0].shape[2] // width
        count = total.shape[1]

        def body(side, slots):
            terms = []
            for k in slots:
                row = rows[side, k]
                at = pl.ds(pl.multiple_of((row % halves) * width, width), width)
                lhs = [part[row // halves, :, at] for part in parts]
                lhs = lhs[0] if part_total == 1 else jnp.concatenate(lhs, axis=0)
                terms.append(jnp.dot(lhs, blocks[side, k], preferred_element_type=jnp.float32))
            for k, term in zip(slots, terms):
                total[cols[side, k]] += term

        steps = each_live(sources, blocks, sems, live, body, 4)
        next(steps)
        total[...] = jnp.zeros_like(total)
        next(steps)
        share = count // len(outs)
        for mask, out in enumerate(outs):
            start = pl.multiple_of((origin[0] ^ mask) * share, share)
            out[...] = total[:, pl.ds(start, share), :].astype(out.dtype)

    return kernel


def make_apply(part_total):
    def kernel(rows, cols, live, origin, *rest):
        parts, rest = rest[:part_total], rest[part_total:]
        sources, outs = rest[:CORES], rest[CORES + 1 : -3]
        blocks, total, sems = rest[-3:]
        width = blocks.shape[2]
        halves = outs[0].shape[2] // width
        count = total.shape[1]

        def body(side, slots):
            terms = []
            for k in slots:
                lhs = jnp.concatenate([part[cols[side, k]] for part in parts], axis=0)
                terms.append(
                    lax.dot_general(
                        lhs,
                        blocks[side, k],
                        (((1,), (1,)), ((), ())),
                        preferred_element_type=jnp.float32,
                    )
                )
            for k, term in zip(slots, terms):
                total[rows[side, k]] += term

        steps = each_live(sources, blocks, sems, live, body, 4)
        next(steps)
        total[...] = jnp.zeros_like(total)
        next(steps)
        share = count // part_total
        for place in range(part_total):
            start = pl.multiple_of((origin[0] ^ place) * share, share)
            out = outs[place % len(outs)]
            to = pl.ds(0 if len(outs) > 1 else place * share, share)
            for row in range(total.shape[0]):
                at = pl.ds((row % halves) * width, width)
                out[row // halves, to, at] = total[row, pl.ds(start, share), :].astype(out.dtype)

    return kernel


def scratch(weights, total_shape):
    slots = weights.shape[0]
    return [
        pltpu.VMEM((CORES,) + weights.shape, weights.dtype),
        pltpu.VMEM(total_shape, jnp.float32),
        pltpu.SemaphoreType.DMA((CORES, 6 if slots % 6 == 0 else 1)),
    ]


def options(weights, count):
    slots, height, width = weights.shape
    return dict(
        compiler_params=pltpu.CompilerParams(vmem_limit_bytes=VMEM_BYTES),
        cost_estimate=pl.CostEstimate(
            flops=2 * CORES * slots * height * width * count,
            bytes_accessed=CORES * weights.size * 2 + 4 * 1024 * 1024,
            transcendentals=0,
        ),
    )


def project(index, parts, weights, after, col_total, parties):
    count = sum(part.shape[1] for part in parts)
    width = weights[0].shape[2]
    kinds = [jnp.float32] + [jnp.bfloat16] * (parties - 1)
    return pl.pallas_call(
        make_project(len(parts)),
        out_shape=[jax.ShapeDtypeStruct((col_total, count // parties, width), k) for k in kinds],
        in_specs=[SCALARS] * 4 + [WHOLE] * len(parts) + [ANYWHERE] * (CORES + 1),
        out_specs=[WHOLE] * parties,
        scratch_shapes=scratch(weights[0], (col_total, count, width)),
        **options(weights[0], count),
    )(*index, *parts, *weights, after)


def apply(index, parts, weights, after, shapes):
    planes, _, points = shapes[0]
    count = sum(shape[1] for shape in shapes)
    height = weights[0].shape[1]
    return pl.pallas_call(
        make_apply(len(parts)),
        out_shape=[jax.ShapeDtypeStruct(shape, jnp.bfloat16) for shape in shapes],
        in_specs=[SCALARS] * 4 + [WHOLE] * len(parts) + [ANYWHERE] * (CORES + 1),
        out_specs=[WHOLE] * len(shapes),
        scratch_shapes=scratch(weights[0], (planes * points // height, count, height)),
        **options(weights[0], count),
    )(*index, *parts, *weights, after)


def per_device(orbitals, projector_blocks, block_rows, block_cols, block_counts, strengths):
    slabs = lax.axis_size("dom")
    parties = lax.axis_size("band")
    chips = slabs // CORES
    local, all_planes, points = orbitals.shape
    planes = all_planes // chips
    weights = projector_blocks[0, 0]
    slots, height, width = weights.shape
    col_blocks = strengths.shape[0] // width
    row_blocks = planes * points // height // CORES
    band = lax.axis_index("band").astype(jnp.int32)
    place = lax.axis_index("dom").astype(jnp.int32)
    core, chip = place % CORES, place // CORES
    direct = DIRECT and chips == parties and all(size % 16 == 0 for size in CHUNKS)
    sizes = CHUNKS if direct and sum(CHUNKS) == local else (local,)

    def across(value, steps):
        return shifted(value, "dom", CORES * steps)

    def bring(piece):
        if direct:
            parts = []
            for mask in range(chips):
                start = (chip ^ mask) * planes
                part = lax.dynamic_slice_in_dim(piece, start, planes, axis=1).transpose(1, 0, 2)
                parts.append(swapped(part, "dom", CORES * mask) if mask else part)
            return parts
        size = piece.shape[0]
        piece = piece.reshape(size, chips, planes, points).transpose(1, 2, 0, 3)
        groups = [[CORES * i + c for i in range(chips)] for c in range(CORES)]
        states = lax.all_to_all(piece, "dom", 0, 0, axis_index_groups=groups, tiled=True)
        return [states.transpose(1, 0, 2, 3).reshape(planes, chips * size, points)]

    def returned(parts, size):
        if direct:
            parts = [parts[0]] + [swapped(part, "dom", CORES * m) for m, part in enumerate(parts) if m]
            whole = jnp.zeros((size, all_planes, points), jnp.bfloat16)
            for mask, part in enumerate(parts):
                start = (chip ^ mask) * planes
                whole = lax.dynamic_update_slice_in_dim(whole, part.transpose(1, 0, 2), start, axis=1)
            return whole
        result = parts[0].reshape(planes, chips, size, points).transpose(1, 0, 2, 3)
        groups = [[CORES * i + c for i in range(chips)] for c in range(CORES)]
        result = lax.all_to_all(result, "dom", 0, 0, axis_index_groups=groups, tiled=True)
        return result.reshape(all_planes, size, points).transpose(1, 0, 2)

    numbers = jnp.concatenate(
        [
            block_rows.reshape(-1).astype(jnp.float32),
            block_cols.reshape(-1).astype(jnp.float32),
            block_counts.reshape(-1).astype(jnp.float32),
            strengths,
        ]
    )
    pair = jnp.stack([numbers, swapped(numbers, "dom", 1)])
    sides = jnp.stack([core, 1 - core])[:, None]
    index = (
        pair[:, :slots].astype(jnp.int32) + sides * row_blocks,
        pair[:, slots : 2 * slots].astype(jnp.int32) + sides * col_blocks,
        pair[:, 2 * slots].astype(jnp.int32),
        (band ^ chip if direct else band).reshape(1),
    )
    scaling = pair[:, 2 * slots + 1 :]
    scaling = jnp.where(core == 0, scaling, scaling[::-1]).reshape(CORES, col_blocks, 1, width)
    both = (weights, swapped(weights, "dom", 1))

    def summed(shares):
        partial = shares[0]
        for mask, share in enumerate(shares[1:], 1):
            partial = partial + swapped(share, "band", mask).astype(jnp.float32)
        return partial.reshape(CORES + 2, col_blocks, *partial.shape[1:])

    def scaled(partial):
        below = across(partial[CORES + 1], 1)
        above = across(partial[0], -1)
        own = [partial[1] + below, partial[CORES] + above]
        return (scaling * jnp.stack(own)).astype(jnp.bfloat16)

    def gathered(chi):
        near = jnp.concatenate([across(chi[CORES - 1 :], 1), chi, across(chi[:1], -1)], axis=0)
        near = near.reshape(-1, *near.shape[2:])
        return [near] + [swapped(near, "band", mask) for mask in range(1, parties)]

    chis, shapes, token = [], [], strengths
    first = 0
    for size in sizes:
        parts = bring(orbitals[first : first + size])
        first += size
        shapes.append([part.shape for part in parts])
        partial = summed(project(index, parts, both, token, (CORES + 2) * col_blocks, parties))
        token = partial
        chis.append(scaled(partial))
    finished = []
    for size, shape, chi in zip(sizes, shapes, chis):
        result = apply(index, gathered(chi), both, chis[-1], shape)
        finished.append(returned(result, size))
    return finished[0] if len(finished) == 1 else jnp.concatenate(finished, axis=0)


def solution(mesh):
    return jax.shard_map(
        per_device,
        mesh=mesh,
        in_specs=(
            P("dom", None, "band"),
            P("band", "dom", None, None, None),
            P("band", "dom", None),
            P("band", "dom", None),
            P("band", "dom"),
            P("dom"),
        ),
        out_specs=P("dom", None, "band"),
        check_vma=False,
    )
```

time: 417 us -> 159 us (0.38)
  waiting for transfers between devices: 179 us -> 62.5 us
  other arithmetic: 76.8 us -> 2.28 us
  starting transfers between devices: 13.5 us -> 70 us
  blocking collectives: 51.5 us -> 0 us
  local copies, waits for them, and re-layouts: 52.7 us -> 4.98 us
  matrix products: 28.7 us -> 0 us
  Pallas kernels: 0 us -> 15.7 us
  between operations: 14.2 us -> 1.05 us
    psum x1 -> x0, waiting for transfers between devices: 92.8 us -> none  [per_device(): summed = lax.psum(partial_value, 'band')]
    scatter-add x2 -> x0, other arithmetic: 72.6 us -> none  [the longest x1 54.2 us: per_device(): placed = jnp.zeros((state_total, row_blocks, row_width), jnp.float32).at[...]
    ppermute x4 -> x34, starting transfers between devices: 7.18 us -> 70 us  [the longest x26 55.1 us: swapped(): return lax.ppermute(value, axis, [(i, i ^ mask) for i in range(count)])]
    all_to_all x1 -> x0, blocking collectives: 51.5 us -> none  [per_device(): lax.all_to_all(result, 'dom', split_axis=0, concat_axis=1, tiled=True)]
    all_to_all x1 -> x0, waiting for transfers between devices: 47.8 us -> none  [per_device(): lax.all_to_all(orbitals, 'dom', split_axis=1, concat_axis=0, tiled=True)]
    dot_general x2 -> x0, matrix products: 28.7 us -> none  [the longest x1 14.4 us: per_device(): jnp.einsum('skr,krc->kcs', picked, weights, preferred_element_type=jnp.fl...]
    ppermute x4 -> x34, waiting for transfers between devices: 38.2 us -> 62.5 us  [the longest x26 57.4 us: swapped(): return lax.ppermute(value, axis, [(i, i ^ mask) for i in range(count)])]
    pallas_call x0 -> x4, Pallas kernels: none -> 15.7 us  [the longest x2 8.25 us: apply(): pl.pallas_call(make_apply(len(parts)), out_shape=[jax.ShapeDtypeStruct(sh...]
  transfers between devices with their start and end apart: 6 -> 34, of which waited for: 4 -> 14; matrix products, arithmetic and copies ran while one was open for 0% -> 4% of each run, Pallas kernels for 0% -> 5%
where the time goes in v1:
time: 159 us; the launch traced here: 156 us
  starting transfers between devices  70 us (44%)
  waiting for transfers between devices  62.5 us (39%)
  Pallas kernels  15.7 us (10%)
  local copies, waits for them, and re-layouts  4.98 us (3%)
  other arithmetic  2.28 us (1%)
    ppermute x26, waiting for transfers between devices, swapped(): return lax.ppermute(value, axis, [(i, i ^ mask) for i in range(count)])  57.4 us
    ppermute x26, starting transfers between devices, swapped(): return lax.ppermute(value, axis, [(i, i ^ mask) for i in range(count)])  55.1 us
    ppermute x8, starting transfers between devices, shifted(): lax.ppermute(value, axis, [(i, (i + steps) % count) for i in range(count)])  14.9 us
    pallas_call x2, Pallas kernels, apply(): pl.pallas_call(make_apply(len(parts)), out_shape=[jax.ShapeDtypeStruct(sh...  8.25 us
    pallas_call x2, Pallas kernels, project(): pl.pallas_call(make_project(len(parts)), out_shape=[jax.ShapeDtypeStruct(...  7.45 us
    ppermute x8, waiting for transfers between devices, shifted(): lax.ppermute(value, axis, [(i, (i + steps) % count) for i in range(count)])  5.09 us
  transfers between devices with their start and end apart: 34, of which 14 were waited for; matrix products, arithmetic and copies ran while one was open for 4% of the time, Pallas kernels for 5%

profile of v1, /device:TPU:0, one launch (start us, length us, event | category | flops | bytes accessed | tf_op | source)
XLA Modules:
  0.0 156.5 jit_solution(146973279106472999)
XLA Ops:
  0.5 1.8 %fusion.9 = (bf16[16,64,512]{2,1,0:T(8,128)(2,1)S(1)}, bf16[16,64,512]{2,1,0:T(8,128)(2,1)S(1)}) fusion(bf16[32,64,512]{2,1,0:T(8,128)(2,1)} %param.6), kind=kLoop, calls=%fused_computation.54 | loop fusion | bytes 4194304 | tf_op jit(solution)/shard_map/slice | solution.py:271
  2.6 2.6 %collective-permute-start.1 = (bf16[16,16,512]{2,1,0:T(8,128)(2,1)S(1)}, bf16[16,16,512]{2,1,0:T(8,128)(2,1)S(1)}, u32[]{:S(2)}, u32[]{:S(2)}) collective-permute-start(bf16[16,16,512]{2,1,0:T(8,128)(2,1)S(1)} %bitcast.76), channel_id=1, source_target_pairs={{0,2},{1,3},{2,0},{3,1},{4,6},{5,7},{6,4},{7,5},{8,10},{9,11},{10,... | collective-permute-start | bytes 786440 | tf_op jit(solution)/shard_map/ppermute | solution.py:24
  5.4 2.7 %collective-permute-start.2 = (bf16[16,16,512]{2,1,0:T(8,128)(2,1)S(1)}, bf16[16,16,512]{2,1,0:T(8,128)(2,1)S(1)}, u32[]{:S(2)}, u32[]{:S(2)}) collective-permute-start(bf16[16,16,512]{2,1,0:T(8,128)(2,1)S(1)} %bitcast.77), channel_id=1, source_target_pairs={{0,4},{1,5},{2,6},{3,7},{4,0},{5,1},{6,2},{7,3},{8,12},{9,13},{10,... | collective-permute-start | bytes 786440 | tf_op jit(solution)/shard_map/ppermute | solution.py:24
  10.5 6.8 %collective-permute-done.1.rest_1_ = bf16[16,16,512]{2,1,0:T(8,128)(2,1)S(1)} collective-permute-done((bf16[16,16,512]{2,1,0:T(8,128)(2,1)S(1)}, bf16[16,16,512]{2,1,0:T(8,128)(2,1)S(1)}, u32[]{:S(2)}, u32[]{:S(2)}) %collective-permute-start.1) | collective-permute-done | bytes 262176 | tf_op jit(solution)/shard_map/ppermute | solution.py:24
  17.3 9.5 %collective-permute-done.2.rest_2_ = bf16[16,16,512]{2,1,0:T(8,128)(2,1)S(1)} collective-permute-done((bf16[16,16,512]{2,1,0:T(8,128)(2,1)S(1)}, bf16[16,16,512]{2,1,0:T(8,128)(2,1)S(1)}, u32[]{:S(2)}, u32[]{:S(2)}) %collective-permute-start.2) | collective-permute-done | bytes 262176 | tf_op jit(solution)/shard_map/ppermute | solution.py:24
  26.8 3.7 %shard_map.64 = (f32[36,16,128]{2,1,0:T(8,128)S(1)}, bf16[36,16,128]{2,1,0:T(8,128)(2,1)S(1)}, bf16[36,16,128]{2,1,0:T(8,128)(2,1)S(1)}, bf16[36,16,128]{2,1,0:T(8,128)(2,1)S(1)}) custom-call(s32[2,96]{1,0:T(2,128)S(1)} %get-tuple-element.58.rows, s32[2,96]{1,0:T(2,128)S(1)} %get-tuple-element.57.cols, s32[2]{0:T(128)S(1)} %fusion.6.live, s32[1]{0:T(128)} %bitcast.5.origin, ...), custom_call_target="tpu_custom_call" | custom-call | flops 805306368 | bytes 16777216 | tf_op jit(solution)/shard_map/pallas_call | solution.py:161
  30.5 5.0 %collective-permute-start.5 = (bf16[36,16,128]{2,1,0:T(8,128)(2,1)S(1)}, bf16[36,16,128]{2,1,0:T(8,128)(2,1)S(1)}, u32[]{:S(2)}, u32[]{:S(2)}) collective-permute-start(bf16[36,16,128]{2,1,0:T(8,128)(2,1)S(1)} %get-tuple-element.22), channel_id=1, source_target_pairs={{0,8},{8,0},{16,24},{24,16},{1,9},{9,1},{17,25},{25,17},{2,10},{10... | collective-permute-start | bytes 442376 | tf_op jit(solution)/shard_map/ppermute | solution.py:24
  35.6 4.5 %collective-permute-start.15 = (bf16[16,16,512]{2,1,0:T(8,128)(2,1)S(1)}, bf16[16,16,512]{2,1,0:T(8,128)(2,1)S(1)}, u32[]{:S(2)}, u32[]{:S(2)}) collective-permute-start(bf16[16,16,512]{2,1,0:T(8,128)(2,1)S(1)} %bitcast.79), channel_id=1, source_target_pairs={{0,2},{1,3},{2,0},{3,1},{4,6},{5,7},{6,4},{7,5},{8,10},{9,11},{10,... | collective-permute-start | bytes 786440 | tf_op jit(solution)/shard_map/ppermute | solution.py:24
  43.7 2.4 %collective-permute-start.6 = (bf16[36,16,128]{2,1,0:T(8,128)(2,1)S(1)}, bf16[36,16,128]{2,1,0:T(8,128)(2,1)S(1)}, u32[]{:S(2)}, u32[]{:S(2)}) collective-permute-start(bf16[36,16,128]{2,1,0:T(8,128)(2,1)S(1)} %get-tuple-element.23), channel_id=1, source_target_pairs={{0,16},{8,24},{16,0},{24,8},{1,17},{9,25},{17,1},{25,9},{2,18},{10... | collective-permute-start | bytes 442376 | tf_op jit(solution)/shard_map/ppermute | solution.py:24
  47.5 4.8 %collective-permute-done.6 = bf16[36,16,128]{2,1,0:T(8,128)(2,1)S(1)} collective-permute-done((bf16[36,16,128]{2,1,0:T(8,128)(2,1)S(1)}, bf16[36,16,128]{2,1,0:T(8,128)(2,1)S(1)}, u32[]{:S(2)}, u32[]{:S(2)}) %collective-permute-start.6) | collective-permute-done | bytes 147488 | tf_op jit(solution)/shard_map/ppermute | solution.py:24
  52.4 9.3 %collective-permute-done.16.rest_2_ = bf16[16,16,512]{2,1,0:T(8,128)(2,1)S(1)} collective-permute-done((bf16[16,16,512]{2,1,0:T(8,128)(2,1)S(1)}, bf16[16,16,512]{2,1,0:T(8,128)(2,1)S(1)}, u32[]{:S(2)}, u32[]{:S(2)}) %collective-permute-start.16) | collective-permute-done | bytes 262176 | tf_op jit(solution)/shard_map/ppermute | solution.py:24
  61.8 3.7 %shard_map.65 = (f32[36,16,128]{2,1,0:T(8,128)S(1)}, bf16[36,16,128]{2,1,0:T(8,128)(2,1)S(1)}, bf16[36,16,128]{2,1,0:T(8,128)(2,1)S(1)}, bf16[36,16,128]{2,1,0:T(8,128)(2,1)S(1)}) custom-call(s32[2,96]{1,0:T(2,128)S(1)} %get-tuple-element.58.rows, s32[2,96]{1,0:T(2,128)S(1)} %get-tuple-element.57.cols, s32[2]{0:T(128)S(1)} %fusion.6.live, s32[1]{0:T(128)} %bitcast.5.origin, ...), custom_call_target="tpu_custom_call" | custom-call | flops 805306368 | bytes 16777216 | tf_op jit(solution)/shard_map/pallas_call | solution.py:161
  65.5 4.0 %collective-permute-start.18 = (bf16[36,16,128]{2,1,0:T(8,128)(2,1)S(1)}, bf16[36,16,128]{2,1,0:T(8,128)(2,1)S(1)}, u32[]{:S(2)}, u32[]{:S(2)}) collective-permute-start(bf16[36,16,128]{2,1,0:T(8,128)(2,1)S(1)} %get-tuple-element.26), channel_id=1, source_target_pairs={{0,8},{8,0},{16,24},{24,16},{1,9},{9,1},{17,25},{25,17},{2,10},{10... | collective-permute-start | bytes 442376 | tf_op jit(solution)/shard_map/ppermute | solution.py:24
  69.5 3.4 %collective-permute-start.19 = (bf16[36,16,128]{2,1,0:T(8,128)(2,1)S(1)}, bf16[36,16,128]{2,1,0:T(8,128)(2,1)S(1)}, u32[]{:S(2)}, u32[]{:S(2)}) collective-permute-start(bf16[36,16,128]{2,1,0:T(8,128)(2,1)S(1)} %get-tuple-element.27), channel_id=1, source_target_pairs={{0,16},{8,24},{16,0},{24,8},{1,17},{9,25},{17,1},{25,9},{2,18},{10... | collective-permute-start | bytes 442376 | tf_op jit(solution)/shard_map/ppermute | solution.py:24
  76.1 2.8 %collective-permute-done.20 = bf16[36,16,128]{2,1,0:T(8,128)(2,1)S(1)} collective-permute-done((bf16[36,16,128]{2,1,0:T(8,128)(2,1)S(1)}, bf16[36,16,128]{2,1,0:T(8,128)(2,1)S(1)}, u32[]{:S(2)}, u32[]{:S(2)}) %collective-permute-start.20) | collective-permute-done | bytes 147488 | tf_op jit(solution)/shard_map/ppermute | solution.py:24
  79.0 2.2 %collective-permute-start.21 = (f32[9,16,128]{2,1,0:T(8,128)S(1)}, f32[9,16,128]{2,1,0:T(8,128)S(1)}, u32[]{:S(2)}, u32[]{:S(2)}) collective-permute-start(f32[9,16,128]{2,1,0:T(8,128)S(1)} %slice.87), channel_id=1, source_target_pairs={{0,2},{1,3},{2,4},{3,5},{4,6},{5,7},{6,0},{7,1},{8,10},{9,11},{10,... | collective-permute-start | bytes 221192 | tf_op jit(solution)/shard_map/ppermute | solution.py:19
  81.3 1.8 %collective-permute-start.9 = (f32[9,16,128]{2,1,0:T(8,128)S(1)}, f32[9,16,128]{2,1,0:T(8,128)S(1)}, u32[]{:S(2)}, u32[]{:S(2)}) collective-permute-start(f32[9,16,128]{2,1,0:T(8,128)S(1)} %get-tuple-element.48), channel_id=1, source_target_pairs={{0,6},{1,7},{2,0},{3,1},{4,2},{5,3},{6,4},{7,5},{8,14},{9,15},{10,... | collective-permute-start | bytes 221192 | tf_op jit(solution)/shard_map/ppermute | solution.py:19
  83.1 2.3 %collective-permute-done.21 = f32[9,16,128]{2,1,0:T(8,128)S(1)} collective-permute-done((f32[9,16,128]{2,1,0:T(8,128)S(1)}, f32[9,16,128]{2,1,0:T(8,128)S(1)}, u32[]{:S(2)}, u32[]{:S(2)}) %collective-permute-start.21) | collective-permute-done | bytes 73760 | tf_op jit(solution)/shard_map/ppermute | solution.py:19
  85.4 2.4 %collective-permute-start.22 = (f32[9,16,128]{2,1,0:T(8,128)S(1)}, f32[9,16,128]{2,1,0:T(8,128)S(1)}, u32[]{:S(2)}, u32[]{:S(2)}) collective-permute-start(f32[9,16,128]{2,1,0:T(8,128)S(1)} %get-tuple-element.50), channel_id=1, source_target_pairs={{0,6},{1,7},{2,0},{3,1},{4,2},{5,3},{6,4},{7,5},{8,14},{9,15},{10,... | collective-permute-start | bytes 221192 | tf_op jit(solution)/shard_map/ppermute | solution.py:19
  87.8 2.8 %collective-permute-done.22 = f32[9,16,128]{2,1,0:T(8,128)S(1)} collective-permute-done((f32[9,16,128]{2,1,0:T(8,128)S(1)}, f32[9,16,128]{2,1,0:T(8,128)S(1)}, u32[]{:S(2)}, u32[]{:S(2)}) %collective-permute-start.22) | collective-permute-done | bytes 73760 | tf_op jit(solution)/shard_map/ppermute | solution.py:19
  90.7 2.9 %collective-permute-start.10 = (bf16[1,9,16,128]{3,2,1,0:T(8,128)(2,1)S(1)}, bf16[1,9,16,128]{3,2,1,0:T(8,128)(2,1)S(1)}, u32[]{:S(2)}, u32[]{:S(2)}) collective-permute-start(bf16[1,9,16,128]{3,2,1,0:T(8,128)(2,1)S(1)} %get-tuple-element.51), channel_id=1, source_target_pairs={{0,2},{1,3},{2,4},{3,5},{4,6},{5,7},{6,0},{7,1},{8,10},{9,11},{10,... | collective-permute-start | bytes 110600 | tf_op jit(solution)/shard_map/ppermute | solution.py:19
  95.6 2.7 %collective-permute-start.27 = (bf16[1,9,16,128]{3,2,1,0:T(8,128)(2,1)S(1)}, bf16[1,9,16,128]{3,2,1,0:T(8,128)(2,1)S(1)}, u32[]{:S(2)}, u32[]{:S(2)}) collective-permute-start(bf16[1,9,16,128]{3,2,1,0:T(8,128)(2,1)S(1)} %get-tuple-element.54), channel_id=1, source_target_pairs={{0,6},{1,7},{2,0},{3,1},{4,2},{5,3},{6,4},{7,5},{8,14},{9,15},{10,... | collective-permute-start | bytes 110600 | tf_op jit(solution)/shard_map/ppermute | solution.py:19
  98.4 1.9 %collective-permute-start.12 = (bf16[36,16,128]{2,1,0:T(8,128)(2,1)S(1)}, bf16[36,16,128]{2,1,0:T(8,128)(2,1)S(1)}, u32[]{:S(2)}, u32[]{:S(2)}) collective-permute-start(bf16[36,16,128]{2,1,0:T(8,128)(2,1)S(1)} %bitcast.59), channel_id=1, source_target_pairs={{0,8},{8,0},{16,24},{24,16},{1,9},{9,1},{17,25},{25,17},{2,10},{10... | collective-permute-start | bytes 442376 | tf_op jit(solution)/shard_map/ppermute | solution.py:24
  102.0 1.9 %collective-permute-start.28 = (bf16[36,16,128]{2,1,0:T(8,128)(2,1)S(1)}, bf16[36,16,128]{2,1,0:T(8,128)(2,1)S(1)}, u32[]{:S(2)}, u32[]{:S(2)}) collective-permute-start(bf16[36,16,128]{2,1,0:T(8,128)(2,1)S(1)} %bitcast.55), channel_id=1, source_target_pairs={{0,8},{8,0},{16,24},{24,16},{1,9},{9,1},{17,25},{25,17},{2,10},{10... | collective-permute-start | bytes 442376 | tf_op jit(solution)/shard_map/ppermute | solution.py:24
  104.2 1.7 %collective-permute-start.30 = (bf16[36,16,128]{2,1,0:T(8,128)(2,1)S(1)}, bf16[36,16,128]{2,1,0:T(8,128)(2,1)S(1)}, u32[]{:S(2)}, u32[]{:S(2)}) collective-permute-start(bf16[36,16,128]{2,1,0:T(8,128)(2,1)S(1)} %bitcast.57), channel_id=1, source_target_pairs={{0,24},{8,16},{16,8},{24,0},{1,25},{9,17},{17,9},{25,1},{2,26},{10... | collective-permute-start | bytes 442376 | tf_op jit(solution)/shard_map/ppermute | solution.py:24
  105.9 1.8 %collective-permute-done.13.rest_2_ = bf16[36,16,128]{2,1,0:T(8,128)(2,1)S(1)} collective-permute-done((bf16[36,16,128]{2,1,0:T(8,128)(2,1)S(1)}, bf16[36,16,128]{2,1,0:T(8,128)(2,1)S(1)}, u32[]{:S(2)}, u32[]{:S(2)}) %collective-permute-start.13) | collective-permute-done | bytes 147488 | tf_op jit(solution)/shard_map/ppermute | solution.py:24
  107.7 4.0 %shard_map.66 = (bf16[16,16,512]{2,1,0:T(8,128)(2,1)S(1)}, bf16[16,16,512]{2,1,0:T(8,128)(2,1)S(1)}, bf16[16,16,512]{2,1,0:T(8,128)(2,1)S(1)}, bf16[16,16,512]{2,1,0:T(8,128)(2,1)S(1)}) custom-call(s32[2,96]{1,0:T(2,128)S(1)} %get-tuple-element.58.rows, s32[2,96]{1,0:T(2,128)S(1)} %get-tuple-element.57.cols, s32[2]{0:T(128)S(1)} %fusion.6.live, ...), custom_call_target="tpu_custom_call" | custom-call | flops 805306368 | bytes 16777216 | tf_op jit(solution)/shard_map/pallas_call | solution.py:175
  111.8 7.5 %collective-permute-start.24 = (bf16[16,16,512]{2,1,0:T(8,128)(2,1)S(1)}, bf16[16,16,512]{2,1,0:T(8,128)(2,1)S(1)}, u32[]{:S(2)}, u32[]{:S(2)}) collective-permute-start(bf16[16,16,512]{2,1,0:T(8,128)(2,1)S(1)} %get-tuple-element.31), channel_id=1, source_target_pairs={{0,4},{1,5},{2,6},{3,7},{4,0},{5,1},{6,2},{7,3},{8,12},{9,13},{10,... | collective-permute-start | bytes 786440 | tf_op jit(solution)/shard_map/ppermute | solution.py:24
  119.3 4.2 %shard_map.67 = (bf16[16,16,512]{2,1,0:T(8,128)(2,1)S(1)}, bf16[16,16,512]{2,1,0:T(8,128)(2,1)S(1)}, bf16[16,16,512]{2,1,0:T(8,128)(2,1)S(1)}, bf16[16,16,512]{2,1,0:T(8,128)(2,1)S(1)}) custom-call(s32[2,96]{1,0:T(2,128)S(1)} %get-tuple-element.58.rows, s32[2,96]{1,0:T(2,128)S(1)} %get-tuple-element.57.cols, s32[2]{0:T(128)S(1)} %fusion.6.live, ...), custom_call_target="tpu_custom_call" | custom-call | flops 805306368 | bytes 16777216 | tf_op jit(solution)/shard_map/pallas_call | solution.py:175
  124.2 9.0 %collective-permute-start.32 = (bf16[16,16,512]{2,1,0:T(8,128)(2,1)S(1)}, bf16[16,16,512]{2,1,0:T(8,128)(2,1)S(1)}, u32[]{:S(2)}, u32[]{:S(2)}) collective-permute-start(bf16[16,16,512]{2,1,0:T(8,128)(2,1)S(1)} %get-tuple-element.35), channel_id=1, source_target_pairs={{0,4},{1,5},{2,6},{3,7},{4,0},{5,1},{6,2},{7,3},{8,12},{9,13},{10,... | collective-permute-start | bytes 786440 | tf_op jit(solution)/shard_map/ppermute | solution.py:24
  135.1 1.9 %collective-permute-done.31 = bf16[16,16,512]{2,1,0:T(8,128)(2,1)S(1)} collective-permute-done((bf16[16,16,512]{2,1,0:T(8,128)(2,1)S(1)}, bf16[16,16,512]{2,1,0:T(8,128)(2,1)S(1)}, u32[]{:S(2)}, u32[]{:S(2)}) %collective-permute-start.31) | collective-permute-done | bytes 262176 | tf_op jit(solution)/shard_map/ppermute | solution.py:24
  137.2 17.4 %collective-permute-done.32 = bf16[16,16,512]{2,1,0:T(8,128)(2,1)S(1)} collective-permute-done((bf16[16,16,512]{2,1,0:T(8,128)(2,1)S(1)}, bf16[16,16,512]{2,1,0:T(8,128)(2,1)S(1)}, u32[]{:S(2)}, u32[]{:S(2)}) %collective-permute-start.32) | collective-permute-done | bytes 262176 | tf_op jit(solution)/shard_map/ppermute | solution.py:24
  (91 shorter events, 20.0 us)
Async XLA Ops:
  0.0 26.8 %collective-permute-start.4 = (bf16[96,256,128]{2,1,0:T(8,128)(2,1)}, bf16[96,256,128]{2,1,0:T(8,128)(2,1)}, u32[]{:S(2)}, u32[]{:S(2)}) collective-permute-start(bf16[96,256,128]{2,1,0:T(8,128)(2,1)} %bitcast.65), channel_id=1, source_target_pairs={{0,1},{1,0},{2,3},{3,2},{4,5},{5,4},{6,7},{7,6},{8,9},{9,8},{10,11... | collective-permute-start | bytes 18874376 | tf_op jit(solution)/shard_map/ppermute | solution.py:24
  2.6 14.7 %collective-permute-start.1 = (bf16[16,16,512]{2,1,0:T(8,128)(2,1)S(1)}, bf16[16,16,512]{2,1,0:T(8,128)(2,1)S(1)}, u32[]{:S(2)}, u32[]{:S(2)}) collective-permute-start(bf16[16,16,512]{2,1,0:T(8,128)(2,1)S(1)} %bitcast.76), channel_id=1, source_target_pairs={{0,2},{1,3},{2,0},{3,1},{4,6},{5,7},{6,4},{7,5},{8,10},{9,11},{10,... | collective-permute-start | bytes 786440 | tf_op jit(solution)/shard_map/ppermute | solution.py:24
  5.4 21.4 %collective-permute-start.2 = (bf16[16,16,512]{2,1,0:T(8,128)(2,1)S(1)}, bf16[16,16,512]{2,1,0:T(8,128)(2,1)S(1)}, u32[]{:S(2)}, u32[]{:S(2)}) collective-permute-start(bf16[16,16,512]{2,1,0:T(8,128)(2,1)S(1)} %bitcast.77), channel_id=1, source_target_pairs={{0,4},{1,5},{2,6},{3,7},{4,0},{5,1},{6,2},{7,3},{8,12},{9,13},{10,... | collective-permute-start | bytes 786440 | tf_op jit(solution)/shard_map/ppermute | solution.py:24
  8.2 18.6 %collective-permute-start.3 = (bf16[16,16,512]{2,1,0:T(8,128)(2,1)S(1)}, bf16[16,16,512]{2,1,0:T(8,128)(2,1)S(1)}, u32[]{:S(2)}, u32[]{:S(2)}) collective-permute-start(bf16[16,16,512]{2,1,0:T(8,128)(2,1)S(1)} %bitcast.78), channel_id=1, source_target_pairs={{0,6},{1,7},{2,4},{3,5},{4,2},{5,3},{6,0},{7,1},{8,14},{9,15},{10,... | collective-permute-start | bytes 786440 | tf_op jit(solution)/shard_map/ppermute | solution.py:24
  30.5 15.6 %collective-permute-start.5 = (bf16[36,16,128]{2,1,0:T(8,128)(2,1)S(1)}, bf16[36,16,128]{2,1,0:T(8,128)(2,1)S(1)}, u32[]{:S(2)}, u32[]{:S(2)}) collective-permute-start(bf16[36,16,128]{2,1,0:T(8,128)(2,1)S(1)} %get-tuple-element.22), channel_id=1, source_target_pairs={{0,8},{8,0},{16,24},{24,16},{1,9},{9,1},{17,25},{25,17},{2,10},{10... | collective-permute-start | bytes 442376 | tf_op jit(solution)/shard_map/ppermute | solution.py:24
  35.6 16.8 %collective-permute-start.15 = (bf16[16,16,512]{2,1,0:T(8,128)(2,1)S(1)}, bf16[16,16,512]{2,1,0:T(8,128)(2,1)S(1)}, u32[]{:S(2)}, u32[]{:S(2)}) collective-permute-start(bf16[16,16,512]{2,1,0:T(8,128)(2,1)S(1)} %bitcast.79), channel_id=1, source_target_pairs={{0,2},{1,3},{2,0},{3,1},{4,6},{5,7},{6,4},{7,5},{8,10},{9,11},{10,... | collective-permute-start | bytes 786440 | tf_op jit(solution)/shard_map/ppermute | solution.py:24
  40.3 21.4 %collective-permute-start.16 = (bf16[16,16,512]{2,1,0:T(8,128)(2,1)S(1)}, bf16[16,16,512]{2,1,0:T(8,128)(2,1)S(1)}, u32[]{:S(2)}, u32[]{:S(2)}) collective-permute-start(bf16[16,16,512]{2,1,0:T(8,128)(2,1)S(1)} %bitcast.80), channel_id=1, source_target_pairs={{0,4},{1,5},{2,6},{3,7},{4,0},{5,1},{6,2},{7,3},{8,12},{9,13},{10,... | collective-permute-start | bytes 786440 | tf_op jit(solution)/shard_map/ppermute | solution.py:24
  42.0 19.7 %collective-permute-start.17 = (bf16[16,16,512]{2,1,0:T(8,128)(2,1)S(1)}, bf16[16,16,512]{2,1,0:T(8,128)(2,1)S(1)}, u32[]{:S(2)}, u32[]{:S(2)}) collective-permute-start(bf16[16,16,512]{2,1,0:T(8,128)(2,1)S(1)} %bitcast.81), channel_id=1, source_target_pairs={{0,6},{1,7},{2,4},{3,5},{4,2},{5,3},{6,0},{7,1},{8,14},{9,15},{10,... | collective-permute-start | bytes 786440 | tf_op jit(solution)/shard_map/ppermute | solution.py:24
  43.7 8.7 %collective-permute-start.6 = (bf16[36,16,128]{2,1,0:T(8,128)(2,1)S(1)}, bf16[36,16,128]{2,1,0:T(8,128)(2,1)S(1)}, u32[]{:S(2)}, u32[]{:S(2)}) collective-permute-start(bf16[36,16,128]{2,1,0:T(8,128)(2,1)S(1)} %get-tuple-element.23), channel_id=1, source_target_pairs={{0,16},{8,24},{16,0},{24,8},{1,17},{9,25},{17,1},{25,9},{2,18},{10... | collective-permute-start | bytes 442376 | tf_op jit(solution)/shard_map/ppermute | solution.py:24
  46.1 6.3 %collective-permute-start.7 = (bf16[36,16,128]{2,1,0:T(8,128)(2,1)S(1)}, bf16[36,16,128]{2,1,0:T(8,128)(2,1)S(1)}, u32[]{:S(2)}, u32[]{:S(2)}) collective-permute-start(bf16[36,16,128]{2,1,0:T(8,128)(2,1)S(1)} %get-tuple-element.24), channel_id=1, source_target_pairs={{0,24},{8,16},{16,8},{24,0},{1,25},{9,17},{17,9},{25,1},{2,26},{10... | collective-permute-start | bytes 442376 | tf_op jit(solution)/shard_map/ppermute | solution.py:24
  65.5 9.7 %collective-permute-start.18 = (bf16[36,16,128]{2,1,0:T(8,128)(2,1)S(1)}, bf16[36,16,128]{2,1,0:T(8,128)(2,1)S(1)}, u32[]{:S(2)}, u32[]{:S(2)}) collective-permute-start(bf16[36,16,128]{2,1,0:T(8,128)(2,1)S(1)} %get-tuple-element.26), channel_id=1, source_target_pairs={{0,8},{8,0},{16,24},{24,16},{1,9},{9,1},{17,25},{25,17},{2,10},{10... | collective-permute-start | bytes 442376 | tf_op jit(solution)/shard_map/ppermute | solution.py:24
  69.5 6.6 %collective-permute-start.19 = (bf16[36,16,128]{2,1,0:T(8,128)(2,1)S(1)}, bf16[36,16,128]{2,1,0:T(8,128)(2,1)S(1)}, u32[]{:S(2)}, u32[]{:S(2)}) collective-permute-start(bf16[36,16,128]{2,1,0:T(8,128)(2,1)S(1)} %get-tuple-element.27), channel_id=1, source_target_pairs={{0,16},{8,24},{16,0},{24,8},{1,17},{9,25},{17,1},{25,9},{2,18},{10... | collective-permute-start | bytes 442376 | tf_op jit(solution)/shard_map/ppermute | solution.py:24
  72.9 6.1 %collective-permute-start.20 = (bf16[36,16,128]{2,1,0:T(8,128)(2,1)S(1)}, bf16[36,16,128]{2,1,0:T(8,128)(2,1)S(1)}, u32[]{:S(2)}, u32[]{:S(2)}) collective-permute-start(bf16[36,16,128]{2,1,0:T(8,128)(2,1)S(1)} %get-tuple-element.28), channel_id=1, source_target_pairs={{0,24},{8,16},{16,8},{24,0},{1,25},{9,17},{17,9},{25,1},{2,26},{10... | collective-permute-start | bytes 442376 | tf_op jit(solution)/shard_map/ppermute | solution.py:24
  74.4 6.9 %collective-permute-start.8 = (f32[9,16,128]{2,1,0:T(8,128)S(1)}, f32[9,16,128]{2,1,0:T(8,128)S(1)}, u32[]{:S(2)}, u32[]{:S(2)}) collective-permute-start(f32[9,16,128]{2,1,0:T(8,128)S(1)} %slice.81), channel_id=1, source_target_pairs={{0,2},{1,3},{2,4},{3,5},{4,6},{5,7},{6,0},{7,1},{8,10},{9,11},{10,... | collective-permute-start | bytes 221192 | tf_op jit(solution)/shard_map/ppermute | solution.py:19
  79.0 6.4 %collective-permute-start.21 = (f32[9,16,128]{2,1,0:T(8,128)S(1)}, f32[9,16,128]{2,1,0:T(8,128)S(1)}, u32[]{:S(2)}, u32[]{:S(2)}) collective-permute-start(f32[9,16,128]{2,1,0:T(8,128)S(1)} %slice.87), channel_id=1, source_target_pairs={{0,2},{1,3},{2,4},{3,5},{4,6},{5,7},{6,0},{7,1},{8,10},{9,11},{10,... | collective-permute-start | bytes 221192 | tf_op jit(solution)/shard_map/ppermute | solution.py:19
  81.3 6.5 %collective-permute-start.9 = (f32[9,16,128]{2,1,0:T(8,128)S(1)}, f32[9,16,128]{2,1,0:T(8,128)S(1)}, u32[]{:S(2)}, u32[]{:S(2)}) collective-permute-start(f32[9,16,128]{2,1,0:T(8,128)S(1)} %get-tuple-element.48), channel_id=1, source_target_pairs={{0,6},{1,7},{2,0},{3,1},{4,2},{5,3},{6,4},{7,5},{8,14},{9,15},{10,... | collective-permute-start | bytes 221192 | tf_op jit(solution)/shard_map/ppermute | solution.py:19
  85.4 5.2 %collective-permute-start.22 = (f32[9,16,128]{2,1,0:T(8,128)S(1)}, f32[9,16,128]{2,1,0:T(8,128)S(1)}, u32[]{:S(2)}, u32[]{:S(2)}) collective-permute-start(f32[9,16,128]{2,1,0:T(8,128)S(1)} %get-tuple-element.50), channel_id=1, source_target_pairs={{0,6},{1,7},{2,0},{3,1},{4,2},{5,3},{6,4},{7,5},{8,14},{9,15},{10,... | collective-permute-start | bytes 221192 | tf_op jit(solution)/shard_map/ppermute | solution.py:19
  90.7 7.7 %collective-permute-start.10 = (bf16[1,9,16,128]{3,2,1,0:T(8,128)(2,1)S(1)}, bf16[1,9,16,128]{3,2,1,0:T(8,128)(2,1)S(1)}, u32[]{:S(2)}, u32[]{:S(2)}) collective-permute-start(bf16[1,9,16,128]{3,2,1,0:T(8,128)(2,1)S(1)} %get-tuple-element.51), channel_id=1, source_target_pairs={{0,2},{1,3},{2,4},{3,5},{4,6},{5,7},{6,0},{7,1},{8,10},{9,11},{10,... | collective-permute-start | bytes 110600 | tf_op jit(solution)/shard_map/ppermute | solution.py:19
  94.5 7.4 %collective-permute-start.26 = (bf16[1,9,16,128]{3,2,1,0:T(8,128)(2,1)S(1)}, bf16[1,9,16,128]{3,2,1,0:T(8,128)(2,1)S(1)}, u32[]{:S(2)}, u32[]{:S(2)}) collective-permute-start(bf16[1,9,16,128]{3,2,1,0:T(8,128)(2,1)S(1)} %get-tuple-element.53), channel_id=1, source_target_pairs={{0,2},{1,3},{2,4},{3,5},{4,6},{5,7},{6,0},{7,1},{8,10},{9,11},{10,... | collective-permute-start | bytes 110600 | tf_op jit(solution)/shard_map/ppermute | solution.py:19
  95.6 6.3 %collective-permute-start.27 = (bf16[1,9,16,128]{3,2,1,0:T(8,128)(2,1)S(1)}, bf16[1,9,16,128]{3,2,1,0:T(8,128)(2,1)S(1)}, u32[]{:S(2)}, u32[]{:S(2)}) collective-permute-start(bf16[1,9,16,128]{3,2,1,0:T(8,128)(2,1)S(1)} %get-tuple-element.54), channel_id=1, source_target_pairs={{0,6},{1,7},{2,0},{3,1},{4,2},{5,3},{6,4},{7,5},{8,14},{9,15},{10,... | collective-permute-start | bytes 110600 | tf_op jit(solution)/shard_map/ppermute | solution.py:19
  98.4 5.8 %collective-permute-start.12 = (bf16[36,16,128]{2,1,0:T(8,128)(2,1)S(1)}, bf16[36,16,128]{2,1,0:T(8,128)(2,1)S(1)}, u32[]{:S(2)}, u32[]{:S(2)}) collective-permute-start(bf16[36,16,128]{2,1,0:T(8,128)(2,1)S(1)} %bitcast.59), channel_id=1, source_target_pairs={{0,8},{8,0},{16,24},{24,16},{1,9},{9,1},{17,25},{25,17},{2,10},{10... | collective-permute-start | bytes 442376 | tf_op jit(solution)/shard_map/ppermute | solution.py:24
  100.3 7.4 %collective-permute-start.13 = (bf16[36,16,128]{2,1,0:T(8,128)(2,1)S(1)}, bf16[36,16,128]{2,1,0:T(8,128)(2,1)S(1)}, u32[]{:S(2)}, u32[]{:S(2)}) collective-permute-start(bf16[36,16,128]{2,1,0:T(8,128)(2,1)S(1)} %bitcast.60), channel_id=1, source_target_pairs={{0,16},{8,24},{16,0},{24,8},{1,17},{9,25},{17,1},{25,9},{2,18},{10... | collective-permute-start | bytes 442376 | tf_op jit(solution)/shard_map/ppermute | solution.py:24
  100.3 7.4 %collective-permute-start.14 = (bf16[36,16,128]{2,1,0:T(8,128)(2,1)S(1)}, bf16[36,16,128]{2,1,0:T(8,128)(2,1)S(1)}, u32[]{:S(2)}, u32[]{:S(2)}) collective-permute-start(bf16[36,16,128]{2,1,0:T(8,128)(2,1)S(1)} %bitcast.61), channel_id=1, source_target_pairs={{0,24},{8,16},{16,8},{24,0},{1,25},{9,17},{17,9},{25,1},{2,26},{10... | collective-permute-start | bytes 442376 | tf_op jit(solution)/shard_map/ppermute | solution.py:24
  102.0 17.3 %collective-permute-start.28 = (bf16[36,16,128]{2,1,0:T(8,128)(2,1)S(1)}, bf16[36,16,128]{2,1,0:T(8,128)(2,1)S(1)}, u32[]{:S(2)}, u32[]{:S(2)}) collective-permute-start(bf16[36,16,128]{2,1,0:T(8,128)(2,1)S(1)} %bitcast.55), channel_id=1, source_target_pairs={{0,8},{8,0},{16,24},{24,16},{1,9},{9,1},{17,25},{25,17},{2,10},{10... | collective-permute-start | bytes 442376 | tf_op jit(solution)/shard_map/ppermute | solution.py:24
  103.9 15.4 %collective-permute-start.29 = (bf16[36,16,128]{2,1,0:T(8,128)(2,1)S(1)}, bf16[36,16,128]{2,1,0:T(8,128)(2,1)S(1)}, u32[]{:S(2)}, u32[]{:S(2)}) collective-permute-start(bf16[36,16,128]{2,1,0:T(8,128)(2,1)S(1)} %bitcast.56), channel_id=1, source_target_pairs={{0,16},{8,24},{16,0},{24,8},{1,17},{9,25},{17,1},{25,9},{2,18},{10... | collective-permute-start | bytes 442376 | tf_op jit(solution)/shard_map/ppermute | solution.py:24
  104.2 15.1 %collective-permute-start.30 = (bf16[36,16,128]{2,1,0:T(8,128)(2,1)S(1)}, bf16[36,16,128]{2,1,0:T(8,128)(2,1)S(1)}, u32[]{:S(2)}, u32[]{:S(2)}) collective-permute-start(bf16[36,16,128]{2,1,0:T(8,128)(2,1)S(1)} %bitcast.57), channel_id=1, source_target_pairs={{0,24},{8,16},{16,8},{24,0},{1,25},{9,17},{17,9},{25,1},{2,26},{10... | collective-permute-start | bytes 442376 | tf_op jit(solution)/shard_map/ppermute | solution.py:24
  111.7 22.0 %collective-permute-start.23 = (bf16[16,16,512]{2,1,0:T(8,128)(2,1)S(1)}, bf16[16,16,512]{2,1,0:T(8,128)(2,1)S(1)}, u32[]{:S(2)}, u32[]{:S(2)}) collective-permute-start(bf16[16,16,512]{2,1,0:T(8,128)(2,1)S(1)} %get-tuple-element.30), channel_id=1, source_target_pairs={{0,2},{1,3},{2,0},{3,1},{4,6},{5,7},{6,4},{7,5},{8,10},{9,11},{10,... | collective-permute-start | bytes 786440 | tf_op jit(solution)/shard_map/ppermute | solution.py:24
  111.8 23.0 %collective-permute-start.24 = (bf16[16,16,512]{2,1,0:T(8,128)(2,1)S(1)}, bf16[16,16,512]{2,1,0:T(8,128)(2,1)S(1)}, u32[]{:S(2)}, u32[]{:S(2)}) collective-permute-start(bf16[16,16,512]{2,1,0:T(8,128)(2,1)S(1)} %get-tuple-element.31), channel_id=1, source_target_pairs={{0,4},{1,5},{2,6},{3,7},{4,0},{5,1},{6,2},{7,3},{8,12},{9,13},{10,... | collective-permute-start | bytes 786440 | tf_op jit(solution)/shard_map/ppermute | solution.py:24
  119.3 15.7 %collective-permute-start.25 = (bf16[16,16,512]{2,1,0:T(8,128)(2,1)S(1)}, bf16[16,16,512]{2,1,0:T(8,128)(2,1)S(1)}, u32[]{:S(2)}, u32[]{:S(2)}) collective-permute-start(bf16[16,16,512]{2,1,0:T(8,128)(2,1)S(1)} %get-tuple-element.32), channel_id=1, source_target_pairs={{0,6},{1,7},{2,4},{3,5},{4,2},{5,3},{6,0},{7,1},{8,14},{9,15},{10,... | collective-permute-start | bytes 786440 | tf_op jit(solution)/shard_map/ppermute | solution.py:24
  123.5 13.5 %collective-permute-start.31 = (bf16[16,16,512]{2,1,0:T(8,128)(2,1)S(1)}, bf16[16,16,512]{2,1,0:T(8,128)(2,1)S(1)}, u32[]{:S(2)}, u32[]{:S(2)}) collective-permute-start(bf16[16,16,512]{2,1,0:T(8,128)(2,1)S(1)} %get-tuple-element.34), channel_id=1, source_target_pairs={{0,2},{1,3},{2,0},{3,1},{4,6},{5,7},{6,4},{7,5},{8,10},{9,11},{10,... | collective-permute-start | bytes 786440 | tf_op jit(solution)/shard_map/ppermute | solution.py:24
  124.2 30.5 %collective-permute-start.32 = (bf16[16,16,512]{2,1,0:T(8,128)(2,1)S(1)}, bf16[16,16,512]{2,1,0:T(8,128)(2,1)S(1)}, u32[]{:S(2)}, u32[]{:S(2)}) collective-permute-start(bf16[16,16,512]{2,1,0:T(8,128)(2,1)S(1)} %get-tuple-element.35), channel_id=1, source_target_pairs={{0,4},{1,5},{2,6},{3,7},{4,0},{5,1},{6,2},{7,3},{8,12},{9,13},{10,... | collective-permute-start | bytes 786440 | tf_op jit(solution)/shard_map/ppermute | solution.py:24
  133.8 21.0 %collective-permute-start.33 = (bf16[16,16,512]{2,1,0:T(8,128)(2,1)S(1)}, bf16[16,16,512]{2,1,0:T(8,128)(2,1)S(1)}, u32[]{:S(2)}, u32[]{:S(2)}) collective-permute-start(bf16[16,16,512]{2,1,0:T(8,128)(2,1)S(1)} %get-tuple-element.36), channel_id=1, source_target_pairs={{0,6},{1,7},{2,4},{3,5},{4,2},{5,3},{6,0},{7,1},{8,14},{9,15},{10,... | collective-permute-start | bytes 786440 | tf_op jit(solution)/shard_map/ppermute | solution.py:24
  (5 other events, 26.1 us)
